TPU v7x, 1024 devices: a whole 4x4x32 slice. The times are simulated.
1024 devices in a mesh: row: 16 (over x, z_hi, core), col: 64 (over y, z_lo).
Axes of the slice: x: 4, y: 4, z: 32 (z_hi: 2, z_lo: 16; z = z_hi * 16 + z_lo), core: 2. Of those that a mesh axis runs over, the one named last changes fastest.
Arguments:
- images: float32 [4096, 1152], P(('row', 'col')), may hold values from -0.1875 to 0.1875
- texts: float32 [4096, 1152], P(('col', 'row')), may hold values from -0.1875 to 0.1875
- log_temp: float32 [1], replicated, may hold values from 1 to 1.6
- bias: float32 [1], replicated, may hold values from -4 to -2
Outputs:
- image_grad: float32 [4096, 1152], P(('row', 'col'))
- text_grad: float32 [4096, 1152], P(('col', 'row'))
- loss: float32 [], replicated
- temp_grad: float32 [], replicated
- bias_grad: float32 [], replicated
All inputs are finite; a program needn't handle non-finite values.
Results may differ from a plain program's by a relative error of at most 0.0041.
Values may be sent and summed in bfloat16 or wider, within the bound.
A program may use at most 32 MiB of HBM per device.

v0:
```python
import jax
import jax.numpy as jnp
from jax import lax
from jax.sharding import PartitionSpec as P


def normalize(values):
    norms = jnp.sqrt(jnp.sum(values * values, axis=-1, keepdims=True) + 1e-06)
    return (values / norms, norms)


def unit_backward(unit, norms, grads):
    along = jnp.sum(unit * grads, axis=-1, keepdims=True)
    return (grads - unit * along) / norms


def on_device(images, texts, log_temp, bias):
    img_unit, img_norm = normalize(images)
    txt_unit, txt_norm = normalize(texts)
    img_low = img_unit.astype(jnp.bfloat16)
    txt_low = txt_unit.astype(jnp.bfloat16)
    temp = jnp.exp(log_temp[0])
    offset = bias[0]
    img_block = lax.all_gather(img_low, "col", axis=0, tiled=True)
    txt_block = lax.all_gather(txt_low, "row", axis=0, tiled=True)
    img_count = img_block.shape[0]
    txt_count = txt_block.shape[0]
    pairs = img_count * lax.axis_size("row")
    row_ids = lax.axis_index("row") * img_count + jnp.arange(img_count, dtype=jnp.int32)
    col_ids = lax.axis_index("col") * txt_count + jnp.arange(txt_count, dtype=jnp.int32)
    scores = lax.dot_general(
        txt_block, img_block, (((1,), (1,)), ((), ())), preferred_element_type=jnp.float32
    )
    logits = temp * scores + offset
    label = jnp.where(col_ids[:, None] == row_ids[None, :], 1.0, -1.0).astype(jnp.float32)
    margin = -label * logits
    dlogit = -label * jax.nn.sigmoid(margin)
    dlogit_low = dlogit.astype(jnp.bfloat16)
    txt_part = jnp.dot(dlogit_low, img_block, preferred_element_type=jnp.float32)
    txt_unit_grad = temp * lax.psum_scatter(txt_part, "row", scatter_dimension=0, tiled=True)
    img_part = lax.dot_general(
        dlogit_low, txt_block, (((0,), (0,)), ((), ())), preferred_element_type=jnp.float32
    )
    img_unit_grad = temp * lax.psum_scatter(img_part, "col", scatter_dimension=0, tiled=True)
    local_terms = (jnp.sum(jax.nn.softplus(margin)), jnp.sum(dlogit * scores), jnp.sum(dlogit))
    loss_acc, slope_acc, shift_acc = lax.psum(
        (local_terms[0], local_terms[1], local_terms[2]), ("row", "col")
    )
    image_grad = unit_backward(img_unit, img_norm, img_unit_grad)
    text_grad = unit_backward(txt_unit, txt_norm, txt_unit_grad)
    scale = 1.0 / (float(pairs) * float(pairs))
    return (image_grad, text_grad, loss_acc * scale, temp * slope_acc * scale, shift_acc * scale)


def solution(mesh):
    in_specs = (P(("row", "col"), None), P(("col", "row"), None), P(), P())
    out_specs = (P(("row", "col"), None), P(("col", "row"), None), P(), P(), P())
    return jax.shard_map(
        on_device, mesh=mesh, in_specs=in_specs, out_specs=out_specs, check_vma=False
    )
```

profile of v0, /device:TPU:1, one launch (start us, length us, event | category | flops | bytes accessed | tf_op | source)
XLA Modules:
  0.0 2300.7 jit_solution(6250044024920003689)
XLA Ops:
  7.2 0.0 all-reduce.8.cloned.1.call-start
  8.6 0.8 multiply_reduce_fusion.3
  9.4 0.9 multiply_reduce_fusion.4
  10.3 0.8 convert_bitcast_fusion.1
  11.1 0.8 convert_bitcast_fusion
  11.9 83.9 %all-gather = bf16[16,4,1152]{2,1,0:T(4,128)(2,1)S(1)} all-gather(bf16[1,4,1152]{2,1,0:T(4,128)(2,1)S(1)} %get-tuple-element.13), channel_id=1, replica_groups=mesh['row'=16,'col'=64] {'row'}, dimensions={0}, use_global_device_ids=true | all-gather | bytes 156672 | tf_op jit(solution)/shard_map/all_gather | solution.py:25
  95.8 362.1 %all-gather.1 = bf16[64,4,1152]{2,1,0:T(4,128)(2,1)S(1)} all-gather(bf16[1,4,1152]{2,1,0:T(4,128)(2,1)S(1)} %get-tuple-element.11), channel_id=1, replica_groups=mesh['row'=16,'col'=64] {'col'}, dimensions={0}, use_global_device_ids=true | all-gather | bytes 599040 | tf_op jit(solution)/shard_map/all_gather | solution.py:24
  457.9 0.1 reshape.36
  458.1 1.0 fusion.5
  459.0 1.0 fusion.1
  460.0 0.0 all-reduce.8.cloned.1.call-update
  460.1 0.0 all-reduce.6.cloned.1.call-start
  460.1 1.5 fusion.3
  461.6 0.0 all-reduce.6.cloned.1.call-update
  461.6 178.5 %all-reduce.2 = (f32[]{:T(128)}, f32[]{:T(128)}, f32[]{:T(128)}) all-reduce(f32[]{:T(128)} %get-tuple-element.7, f32[]{:T(128)} %get-tuple-element.6, f32[]{:T(128)} %get-tuple-element.5), channel_id=1, replica_groups=mesh['row'=16,'col'=64] {'row','col'}, use_global_device_ids=true, to_apply=%region_7.8 | all-reduce | flops 3 | bytes 24 | tf_op jit(solution)/shard_map/psum | solution.py:46
  640.2 1.3 dynamic-slice.2
  641.4 1.3 dynamic-slice
  645.9 230.6 %all-reduce.8.cloned.1.call-done = f32[64,1152]{1,0:T(8,128)} async-done(((f32[64,1152]{1,0:T(8,128)}), f32[64,1152]{1,0:T(8,128)}) %all-reduce.8.cloned.1.call-update) | async-done | bytes 294928
  876.6 0.9 multiply_reduce_fusion.1
  877.5 1.5 subtract_divide_fusion
  878.9 1409.2 %all-reduce.6.cloned.1.call-done = f32[256,1152]{1,0:T(8,128)} async-done(((f32[256,1152]{1,0:T(8,128)}), f32[256,1152]{1,0:T(8,128)}) %all-reduce.6.cloned.1.call-update) | async-done | bytes 1179664
  2288.1 0.9 multiply_reduce_fusion.2
  2289.0 1.5 subtract_divide_fusion.1
  (5 shorter events, 0.1 us)
Async XLA Ops:
  7.2 869.4 %all-reduce.8.cloned.1.call-start = ((), (), s32[]{:S(2)}) async-start(), calls=%async_computation.1 | async-start | bytes 589824
  460.1 1828.0 %all-reduce.6.cloned.1.call-start = ((), (), s32[]{:S(2)}) async-start(), calls=%async_computation | async-start | bytes 2359296
Sparse Core Ops, SparseCore 0:
  460.2 416.3 all-reduce.7
  880.5 1407.5 all-reduce.5
where the time goes:
time: 2340 us; the launch traced here: 2300 us
  waiting for transfers between devices  1640 us (70%)
  blocking collectives  625 us (27%)
    unnamed x4, waiting for transfers between devices  1640 us
    all_gather x1, blocking collectives, on_device(): img_block = lax.all_gather(img_low, 'col', axis=0, tiled=True)  362 us
    psum x1, blocking collectives, on_device(): lax.psum((local_terms[0], local_terms[1], local_terms[2]), ('row', 'col'))  179 us
    all_gather x1, blocking collectives, on_device(): txt_block = lax.all_gather(txt_low, 'row', axis=0, tiled=True)  83.9 us
  transfers between devices with their start and end apart: 2, of which 2 were waited for; matrix products, arithmetic and copies ran while one was open for 0% of the time, Pallas kernels for 0%

commit v1 on v0

v1 whole, which is shorter than its diff:
```python
import functools

import jax
import jax.numpy as jnp
from jax import lax
from jax.experimental import pallas as pl
from jax.experimental.pallas import tpu as pltpu
from jax.sharding import PartitionSpec as P

MESH = pl.DeviceIdType.MESH
F32 = jnp.float32
BF16 = jnp.bfloat16

FACTORS = dict(nx=4, nzh=2, nc=2, ny=4, nzl=16, run=8)


def remote(src, dst, send, recv, dev):
    return pltpu.make_async_remote_copy(
        src_ref=src, dst_ref=dst, send_sem=send, recv_sem=recv, device_id=dev, device_id_type=MESH
    )


def kernel(
    nx, nzh, nc, ny, nzl, run,
    images, texts, log_temp, bias,
    image_grad, text_grad, terms,
    unit, norm, img_all, txt_all, img_out, txt_out, img_in, txt_in,
    img_zout, txt_zout, img_zin, txt_zin, sc_yc, sc_x, sc_zr, sc_zs,
    s_iz, r_iz, s_tz, r_tz, s_ix, r_ix, s_ty, r_ty,
    s_bx, r_bx, s_by, r_by, s_bi, r_bi, s_bt, r_bt,
    s_ay, r_ay, s_ax, r_ax, s_ar, r_ar, s_as, r_as,
):
    own, width = images.shape
    cut = nzl // run
    nzs = nzh * cut
    nyc = ny * nc
    row, col = lax.axis_index("row"), lax.axis_index("col")
    x, zh, core = row // (nzh * nc), (row // nc) % nzh, row % nc
    y, zl = col // nzl, col % nzl
    zr, zs, yc = zl % run, zh * cut + zl // run, y * nc + core

    def device(x_, y_, core_, zs_, zr_):
        return ((x_ * nzh + zs_ // cut) * nc + core_, y_ * nzl + (zs_ % cut) * run + zr_)

    def on_zr(k):
        to = lax.rem(zr + k, run)
        return to, device(x, y, core, zs, to)

    def on_zs(k):
        to = lax.rem(zs + k, nzs)
        return to, device(x, y, core, to, zr)

    def on_x(k):
        to = lax.rem(x + k, nx)
        return to, device(to, y, core, zs, zr)

    def on_yc(k):
        to = lax.rem(yc + k, nyc)
        return to, device(x, to // nc, lax.rem(to, nc), zs, zr)

    groups = ((on_zs, nzs), (on_yc, nyc), (on_x, nx), (on_zr, run))
    barrier = pltpu.get_barrier_semaphore()
    for peer, count in groups:
        for k in range(1, count):
            pl.semaphore_signal(barrier, inc=1, device_id=peer(k)[1], device_id_type=MESH)

    temp = jnp.exp(jnp.full((1, 1), log_temp[0], F32))
    offset = bias[0]
    for at, values, slot in ((0, images, img_all.at[x, zr]), (1, texts, txt_all.at[yc, zs])):
        v = values[...]
        n = jnp.sqrt(jnp.sum(v * v, axis=-1, keepdims=True) + 1e-06)
        u = v / n
        norm[at] = n
        unit[at] = u
        slot[...] = u.astype(BF16)

    pl.semaphore_wait(barrier, sum(count - 1 for _, count in groups))
    pending = []

    def spread(peer, count, source, target, send, recv):
        for k in range(1, count):
            to, dev = peer(k)
            copy = remote(source(to), target, send.at[to], recv, dev)
            copy.start()
            pending.append(copy)

    def arrive(peer, count, slot, recv):
        for k in range(1, count):
            to, dev = peer(k)
            remote(slot(to), slot(to), recv.at[to], recv.at[to], dev).wait_recv()

    mine_i, mine_t = img_all.at[x, zr], txt_all.at[yc, zs]
    spread(on_zs, nzs, lambda to: mine_t, mine_t, s_tz, r_tz.at[zs])
    spread(on_zr, run, lambda to: mine_i, mine_i, s_iz, r_iz.at[zr])
    arrive(on_zs, nzs, lambda to: txt_all.at[yc, to], r_tz)
    spread(on_yc, nyc, lambda to: txt_all.at[yc], txt_all.at[yc], s_ty, r_ty.at[yc])
    arrive(on_zr, run, lambda to: img_all.at[x, to], r_iz)
    spread(on_x, nx, lambda to: img_all.at[x], img_all.at[x], s_ix, r_ix.at[x])
    arrive(on_yc, nyc, lambda to: txt_all.at[to], r_ty)
    arrive(on_x, nx, lambda to: img_all.at[to], r_ix)

    n_img, n_txt = nx * run * own, nyc * nzs * own
    img = img_all[...].astype(F32).reshape(n_img, width).astype(BF16)
    txt = txt_all[...].astype(F32).reshape(n_txt, width).astype(BF16)
    scores = lax.dot_general(txt, img, (((1,), (1,)), ((), ())), preferred_element_type=F32)
    at_i = lax.broadcasted_iota(jnp.int32, (1, n_img), 1)
    at_t = lax.broadcasted_iota(jnp.int32, (n_txt, 1), 0)
    i_row, i_col = device(at_i // (run * own), y, core, zs, (at_i // own) % run)
    t_yc = at_t // (nzs * own)
    t_row, t_col = device(x, t_yc // nc, t_yc % nc, (at_t // own) % nzs, zr)
    rows, cols = nx * nzh * nc, ny * nzl
    i_id = (i_row * cols + i_col) * own + at_i % own
    t_id = (t_col * rows + t_row) * own + at_t % own
    same = i_id == t_id
    logits = temp * scores + offset
    margin = jnp.where(same, -logits, logits)
    e = jnp.exp(-jnp.abs(margin))
    sig = jnp.where(margin >= 0, 1.0, e) / (1.0 + e)
    dlogit = jnp.where(same, -sig, sig)
    loss = jnp.maximum(margin, 0.0) + jnp.log1p(e)

    def total(v):
        return jnp.sum(jnp.sum(v, axis=0, keepdims=True), axis=1, keepdims=True)

    lane = lax.broadcasted_iota(jnp.int32, (1, 128), 1)
    sums = jnp.where(
        lane == 0, total(loss), jnp.where(lane == 1, total(dlogit * scores), total(dlogit))
    )
    low = dlogit.astype(BF16)

    sc_yc[yc] = sums
    spread(on_yc, nyc, lambda to: sc_yc.at[yc], sc_yc.at[yc], s_ay, r_ay.at[yc])

    txt_part = jnp.dot(low, img, preferred_element_type=F32)
    txt_out[...] = txt_part.reshape(nyc, nzs, own, width).astype(BF16)
    spread(on_yc, nyc, lambda to: txt_out.at[to], txt_in.at[yc], s_by, r_by.at[yc])
    img_part = lax.dot_general(low, txt, (((0,), (0,)), ((), ())), preferred_element_type=F32)
    img_out[...] = img_part.reshape(nx, run, own, width).astype(BF16)
    spread(on_x, nx, lambda to: img_out.at[to], img_in.at[x], s_bx, r_bx.at[x])

    txt_in[yc] = txt_out[yc]
    img_in[x] = img_out[x]

    arrive(on_yc, nyc, lambda to: sc_yc.at[to], r_ay)
    sc_x[x] = jnp.sum(sc_yc[...], axis=0)
    spread(on_x, nx, lambda to: sc_x.at[x], sc_x.at[x], s_ax, r_ax.at[x])

    arrive(on_yc, nyc, lambda to: txt_in.at[to], r_by)
    txt_zout[...] = jnp.sum(txt_in[...].astype(F32), axis=0).astype(BF16)
    spread(on_zs, nzs, lambda to: txt_zout.at[to], txt_zin.at[zs], s_bt, r_bt.at[zs])
    txt_zin[zs] = txt_zout[zs]

    arrive(on_x, nx, lambda to: sc_x.at[to], r_ax)
    sc_zr[zr] = jnp.sum(sc_x[...], axis=0)
    spread(on_zr, run, lambda to: sc_zr.at[zr], sc_zr.at[zr], s_ar, r_ar.at[zr])

    arrive(on_x, nx, lambda to: img_in.at[to], r_bx)
    img_zout[...] = jnp.sum(img_in[...].astype(F32), axis=0).astype(BF16)
    spread(on_zr, run, lambda to: img_zout.at[to], img_zin.at[zr], s_bi, r_bi.at[zr])
    img_zin[zr] = img_zout[zr]

    arrive(on_zr, run, lambda to: sc_zr.at[to], r_ar)
    sc_zs[zs] = jnp.sum(sc_zr[...], axis=0)
    spread(on_zs, nzs, lambda to: sc_zs.at[zs], sc_zs.at[zs], s_as, r_as.at[zs])

    def finish(at, gathered, out):
        g = temp * jnp.sum(gathered[...].astype(F32), axis=0)
        u = unit[at]
        along = jnp.sum(u * g, axis=-1, keepdims=True)
        out[...] = (g - u * along) / norm[at]

    arrive(on_zs, nzs, lambda to: txt_zin.at[to], r_bt)
    finish(1, txt_zin, text_grad)
    arrive(on_zr, run, lambda to: img_zin.at[to], r_bi)
    finish(0, img_zin, image_grad)

    arrive(on_zs, nzs, lambda to: sc_zs.at[to], r_as)
    pairs = float(rows * cols * own)
    scale = 1.0 / (pairs * pairs)
    result = jnp.sum(sc_zs[...], axis=0) * scale
    terms[...] = jnp.where(lane == 1, temp, 1.0) * result
    for copy in pending:
        copy.wait_send()


def on_device(factors, images, texts, log_temp, bias):
    nx, nzh, nc, ny, nzl, run = (factors[k] for k in ("nx", "nzh", "nc", "ny", "nzl", "run"))
    nzs, nyc = nzh * nzl // run, ny * nc
    own, width = images.shape
    vmem = pl.BlockSpec(memory_space=pltpu.VMEM)
    smem = pl.BlockSpec(memory_space=pltpu.SMEM)

    def low(*lead):
        return pltpu.VMEM(lead + (own, width), BF16)

    def sems(*counts):
        out = []
        for c in counts:
            out += [pltpu.SemaphoreType.DMA((c,)), pltpu.SemaphoreType.DMA((c,))]
        return out

    image_grad, text_grad, terms = pl.pallas_call(
        functools.partial(kernel, nx, nzh, nc, ny, nzl, run),
        out_shape=(
            jax.ShapeDtypeStruct((own, width), F32),
            jax.ShapeDtypeStruct((own, width), F32),
            jax.ShapeDtypeStruct((1, 128), F32),
        ),
        in_specs=[vmem, vmem, smem, smem],
        out_specs=(vmem, vmem, vmem),
        scratch_shapes=[
            pltpu.VMEM((2, own, width), F32),
            pltpu.VMEM((2, own, 1), F32),
            low(nx, run), low(nyc, nzs),
            low(nx, run), low(nyc, nzs), low(nx, run), low(nyc, nzs),
            low(run), low(nzs), low(run), low(nzs),
            pltpu.VMEM((nyc, 1, 128), F32),
            pltpu.VMEM((nx, 1, 128), F32),
            pltpu.VMEM((run, 1, 128), F32),
            pltpu.VMEM((nzs, 1, 128), F32),
        ] + sems(run, nzs, nx, nyc, nx, nyc, run, nzs, nyc, nx, run, nzs),
        compiler_params=pltpu.CompilerParams(
            collective_id=0, has_side_effects=True, vmem_limit_bytes=32 * 1024 * 1024
        ),
    )(images, texts, log_temp, bias)
    return image_grad, text_grad, terms[0, 0], terms[0, 1], terms[0, 2]


def solution(mesh, factors=FACTORS):
    in_specs = (P(("row", "col"), None), P(("col", "row"), None), P(), P())
    out_specs = (P(("row", "col"), None), P(("col", "row"), None), P(), P(), P())
    return jax.shard_map(
        functools.partial(on_device, factors),
        mesh=mesh, in_specs=in_specs, out_specs=out_specs, check_vma=False,
    )
```

time: 2340 us -> 80 us (0.03); the launches traced: 2300 us -> 79.8 us
  waiting for transfers between devices: 1640 us -> 0 us
  blocking collectives: 625 us -> 0 us
  Pallas kernels: 0 us -> 74.6 us
    unnamed x4 -> x0, waiting for transfers between devices: 1640 us -> none
    all_gather x2 -> x0, blocking collectives: 446 us -> none  [the longest x1 362 us: on_device(): img_block = lax.all_gather(img_low, 'col', axis=0, tiled=True)]
    psum x1 -> x0, blocking collectives: 179 us -> none  [on_device(): lax.psum((local_terms[0], local_terms[1], local_terms[2]), ('row', 'col'))]
    pallas_call x0 -> x1, Pallas kernels: none -> 74.6 us  [on_device(): pl.pallas_call(functools.partial(kernel, nx, nzh, nc, ny, nzl, run), out_...]
  transfers between devices with their start and end apart: 2 -> 0, of which waited for: 2 -> 0; matrix products, arithmetic and copies ran while one was open for 0% -> 0% of each run, Pallas kernels for 0% -> 0%
where the time goes in v1:
time: 80 us; the launch traced here: 79.8 us
  Pallas kernels  74.6 us (93%)
  local copies, waits for them, and re-layouts  3.24 us (4%)
  between operations  1.94 us (2%)
    pallas_call x1, Pallas kernels, on_device(): pl.pallas_call(functools.partial(kernel, nx, nzh, nc, ny, nzl, run), out_...  74.6 us
    unnamed x6, local copies, waits for them, and re-layouts  2.65 us

profile of v1, /device:TPU:1, one launch (start us, length us, event | category | flops | bytes accessed | tf_op | source)
XLA Modules:
  0.0 79.8 jit_solution(15980996532589038126)
XLA Ops:
  1.9 0.0 copy-start
  1.9 0.7 copy-done
  2.6 0.0 copy-start.1
  2.6 0.7 copy-done.1
  3.4 74.6 %shard_map.83 = (f32[4,1152]{1,0:T(4,128)S(1)}, f32[4,1152]{1,0:T(4,128)S(1)}, f32[1,128]{1,0:T(1,128)S(1)}) custom-call(f32[4,1152]{1,0:T(4,128)S(1)} %copy-done, f32[4,1152]{1,0:T(4,128)S(1)} %copy-done.1, f32[1]{0:T(128)S(6)} %copy.11.log_temp, f32[1]{0:T(128)S(6)} %copy.12.bias), custom_call_target="tpu_custom_call" | custom-call | tf_op jit(solution)/shard_map/pallas_call | solution.py:202
  78.0 0.6 fusion
  78.6 0.6 copy.13
  79.2 0.6 copy.14
Async XLA Ops:
  1.9 0.7 copy-start
  2.6 0.7 copy-start.1

commit v2 on v1

v2 whole, which is shorter than its diff:
```python
import functools

import jax
import jax.numpy as jnp
from jax import lax
from jax.experimental import pallas as pl
from jax.experimental.pallas import tpu as pltpu
from jax.sharding import PartitionSpec as P

MESH = pl.DeviceIdType.MESH
F32 = jnp.float32
BF16 = jnp.bfloat16

FACTORS = dict(
    nx=4, nzh=2, nc=2, ny=4, nzl=16,
    img_to=(9, -8, 8, -7), txt_to=(7, -7, 5, -5, 3, -3, 1, -1),
)


def remote(src, dst, send, recv, dev):
    return pltpu.make_async_remote_copy(
        src_ref=src, dst_ref=dst, send_sem=send, recv_sem=recv, device_id=dev, device_id_type=MESH
    )


def kernel(
    nx, nzh, nc, ny, nzl, img_to, txt_to,
    images, texts, log_temp, bias,
    image_grad, text_grad, terms,
    raw, unit, norm, img_own, txt_own, img_all, txt_all, img_out, txt_out, img_in, txt_in,
    img_zout, txt_zout, img_zin, txt_zin, sc_near, sc_z, load_sem,
    s_iz, r_iz, s_tz, r_tz, s_ix, r_ix, s_ty, r_ty,
    s_bx, r_bx, s_by, r_by, s_bi, r_bi, s_bt, r_bt, s_sn, r_sn, s_sz, r_sz,
):
    own, width = images.shape
    nz, nxc, nq = nzh * nzl, nx * nc, nx * ny * nc
    na, nb = len(img_to), len(txt_to)
    row, col = lax.axis_index("row"), lax.axis_index("col")
    x, zh, core = row // (nzh * nc), (row // nc) % nzh, row % nc
    y, zl = col // nzl, col % nzl
    z, xc, q = zh * nzl + zl, x * nc + core, (x * ny + y) * nc + core

    def device(x_, y_, core_, z_):
        return ((x_ * nzh + z_ // nzl) * nc + core_, y_ * nzl + z_ % nzl)

    def at_z(step):
        return device(x, y, core, lax.rem(z + (step + nz), nz))

    def at_xc(k):
        to = lax.rem(xc + k, nxc)
        return to, device(to // nc, y, lax.rem(to, nc), z)

    def at_y(k):
        to = lax.rem(y + k, ny)
        return to, device(x, to, core, z)

    z_steps = sorted({s % nz for a in img_to + txt_to for s in (a, -a)}, key=lambda s: -min(s, nz - s))
    greeted = [at_z(s) for s in z_steps]
    greeted += [at_y(k)[1] for k in range(1, ny)] + [at_xc(k)[1] for k in range(1, nxc)]
    barrier = pltpu.get_barrier_semaphore()
    for dev in greeted:
        pl.semaphore_signal(barrier, inc=1, device_id=dev, device_id_type=MESH)

    loads = [
        pltpu.make_async_copy(ref, raw.at[at], load_sem.at[at])
        for at, ref in enumerate((images, texts))
    ]
    for load in loads:
        load.start()
    temp = jnp.exp(jnp.full((1, 1), log_temp[0], F32))
    offset = bias[0]
    for at, slot in ((0, img_own), (1, txt_own)):
        loads[at].wait()
        v = raw[at]
        n = jnp.sqrt(jnp.sum(v * v, axis=-1, keepdims=True) + 1e-06)
        u = v / n
        norm[at] = n
        unit[at] = u
        slot[...] = u.astype(BF16)
    pl.semaphore_wait(barrier, len(greeted))

    pending = []

    def send(src, dst, s_sem, r_sem, dev):
        copy = remote(src, dst, s_sem, r_sem, dev)
        copy.start()
        pending.append(copy)

    def arrived(slot, sem):
        remote(slot, slot, sem, sem, at_z(1)).wait_recv()

    trips = [(abs(a), 0, i, a) for i, a in enumerate(img_to)] + [(abs(b), 1, i, b) for i, b in enumerate(txt_to)]
    for _, kind, i, step in sorted(trips, key=lambda t: -t[0]):
        if kind == 0:
            send(img_own, img_all.at[xc, i], s_iz.at[i], r_iz.at[i], at_z(step))
        else:
            send(txt_own, txt_all.at[y, i], s_tz.at[i], r_tz.at[i], at_z(step))
    for i in range(nb):
        arrived(txt_all.at[y, i], r_tz.at[i])
    for k in range(1, ny):
        to, dev = at_y(k)
        send(txt_all.at[y], txt_all.at[y], s_ty.at[to], r_ty.at[y], dev)
    for i in range(na):
        arrived(img_all.at[xc, i], r_iz.at[i])
    for k in range(1, nxc):
        to, dev = at_xc(k)
        send(img_all.at[xc], img_all.at[xc], s_ix.at[to], r_ix.at[xc], dev)
    for k in range(1, ny):
        to, _ = at_y(k)
        arrived(txt_all.at[to], r_ty.at[to])
    for k in range(1, nxc):
        to, _ = at_xc(k)
        arrived(img_all.at[to], r_ix.at[to])

    n_img, n_txt = nxc * na * own, ny * nb * own
    img = img_all[...].astype(F32).reshape(n_img, width).astype(BF16)
    txt = txt_all[...].astype(F32).reshape(n_txt, width).astype(BF16)
    scores = lax.dot_general(txt, img, (((1,), (1,)), ((), ())), preferred_element_type=F32)
    at_i = lax.broadcasted_iota(jnp.int32, (1, n_img), 1)
    at_t = lax.broadcasted_iota(jnp.int32, (n_txt, 1), 0)

    def stepped(steps, index):
        value = jnp.zeros_like(index)
        for i, s in enumerate(steps):
            value = jnp.where(index == i, s, value)
        return value

    i_xc, i_z = at_i // (na * own), (z + nz - stepped(img_to, (at_i // own) % na)) % nz
    t_y, t_z = at_t // (nb * own), (z + nz - stepped(txt_to, (at_t // own) % nb)) % nz
    i_row, i_col = device(i_xc // nc, y, i_xc % nc, i_z)
    t_row, t_col = device(x, t_y, core, t_z)
    rows, cols = nx * nzh * nc, ny * nzl
    i_id = (i_row * cols + i_col) * own + at_i % own
    t_id = (t_col * rows + t_row) * own + at_t % own
    same = i_id == t_id
    logits = temp * scores + offset
    margin = jnp.where(same, -logits, logits)
    e = jnp.exp(-jnp.abs(margin))
    sig = jnp.where(margin >= 0, 1.0, e) / (1.0 + e)
    dlogit = jnp.where(same, -sig, sig)
    loss = jnp.maximum(margin, 0.0) + jnp.log1p(e)

    def total(v):
        return jnp.sum(jnp.sum(v, axis=0, keepdims=True), axis=1, keepdims=True)

    lane = lax.broadcasted_iota(jnp.int32, (1, 128), 1)
    sc_near[q] = jnp.where(
        lane == 0, total(loss), jnp.where(lane == 1, total(dlogit * scores), total(dlogit))
    )
    for k in range(1, nq):
        to = lax.rem(q + k, nq)
        dev = device(to // (ny * nc), (to // nc) % ny, lax.rem(to, nc), z)
        remote(sc_near.at[q], sc_near.at[q], s_sn, r_sn, dev).start()

    low = dlogit.astype(BF16)
    txt_part = jnp.dot(low, img, preferred_element_type=F32)
    txt_out[...] = txt_part.reshape(ny, nb, own, width).astype(BF16)
    for k in range(1, ny):
        to, dev = at_y(k)
        send(txt_out.at[to], txt_in.at[y], s_by.at[to], r_by.at[y], dev)
    img_part = lax.dot_general(low, txt, (((0,), (0,)), ((), ())), preferred_element_type=F32)
    img_out[...] = img_part.reshape(nxc, na, own, width).astype(BF16)
    for k in range(1, nxc):
        to, dev = at_xc(k)
        send(img_out.at[to], img_in.at[xc], s_bx.at[to], r_bx.at[xc], dev)

    remote(sc_near.at[pl.ds(0, nq - 1)], sc_near.at[pl.ds(0, nq - 1)], s_sn, r_sn, at_z(1)).wait_recv()
    sc_z[z] = jnp.sum(sc_near[...], axis=0)
    for k in sorted(range(1, nz), key=lambda s: -min(s, nz - s)):
        remote(sc_z.at[z], sc_z.at[z], s_sz, r_sz, at_z(k)).start()

    acc = txt_out[y].astype(F32)
    for k in range(1, ny):
        to, _ = at_y(k)
        arrived(txt_in.at[to], r_by.at[to])
        acc += txt_in[to].astype(F32)
    txt_zout[...] = acc.astype(BF16)
    for i, b in enumerate(txt_to):
        send(txt_zout.at[i], txt_zin.at[i], s_bt.at[i], r_bt.at[i], at_z(-b))
    acc = img_out[xc].astype(F32)
    for k in range(1, nxc):
        to, _ = at_xc(k)
        arrived(img_in.at[to], r_bx.at[to])
        acc += img_in[to].astype(F32)
    img_zout[...] = acc.astype(BF16)
    for i, a in enumerate(img_to):
        send(img_zout.at[i], img_zin.at[i], s_bi.at[i], r_bi.at[i], at_z(-a))

    def finish(at, gathered, sem, out):
        for i in range(gathered.shape[0]):
            arrived(gathered.at[i], sem.at[i])
        g = temp * jnp.sum(gathered[...].astype(F32), axis=0)
        u = unit[at]
        along = jnp.sum(u * g, axis=-1, keepdims=True)
        out[...] = (g - u * along) / norm[at]

    finish(1, txt_zin, r_bt, text_grad)
    finish(0, img_zin, r_bi, image_grad)

    for copy in pending:
        copy.wait_send()
    rest = sc_near.at[pl.ds(0, nq - 1)]
    remote(rest, rest, s_sn, r_sn, at_z(1)).wait_send()
    rest = sc_z.at[pl.ds(0, nz - 1)]
    remote(rest, rest, s_sz, r_sz, at_z(1)).wait_send()
    remote(rest, rest, s_sz, r_sz, at_z(1)).wait_recv()
    pairs = float(rows * cols * own)
    scale = 1.0 / (pairs * pairs)
    result = jnp.sum(sc_z[...], axis=0) * scale
    terms[...] = jnp.where(lane == 1, temp, 1.0) * result


def on_device(factors, images, texts, log_temp, bias):
    nx, nzh, nc, ny, nzl, img_to, txt_to = (
        factors[k] for k in ("nx", "nzh", "nc", "ny", "nzl", "img_to", "txt_to")
    )
    nxc, na, nb = nx * nc, len(img_to), len(txt_to)
    own, width = images.shape
    vmem = pl.BlockSpec(memory_space=pltpu.VMEM)
    smem = pl.BlockSpec(memory_space=pltpu.SMEM)
    hbm = pl.BlockSpec(memory_space=pl.ANY)

    def low(*lead):
        return pltpu.VMEM(lead + (own, width), BF16)

    def sems(*counts):
        return [pltpu.SemaphoreType.DMA((c,)) for c in counts for _ in range(2)]

    image_grad, text_grad, terms = pl.pallas_call(
        functools.partial(kernel, nx, nzh, nc, ny, nzl, img_to, txt_to),
        out_shape=(
            jax.ShapeDtypeStruct((own, width), F32),
            jax.ShapeDtypeStruct((own, width), F32),
            jax.ShapeDtypeStruct((1, 128), F32),
        ),
        in_specs=[hbm, hbm, smem, smem],
        out_specs=(vmem, vmem, vmem),
        scratch_shapes=[
            pltpu.VMEM((2, own, width), F32),
            pltpu.VMEM((2, own, width), F32),
            pltpu.VMEM((2, own, 1), F32),
            low(), low(),
            low(nxc, na), low(ny, nb),
            low(nxc, na), low(ny, nb), low(nxc, na), low(ny, nb),
            low(na), low(nb), low(na), low(nb),
            pltpu.VMEM((nx * ny * nc, 1, 128), F32),
            pltpu.VMEM((nzh * nzl, 1, 128), F32),
            pltpu.SemaphoreType.DMA((2,)),
        ] + sems(na, nb, nxc, ny, nxc, ny, na, nb) + [pltpu.SemaphoreType.DMA] * 4,
        compiler_params=pltpu.CompilerParams(
            collective_id=0, has_side_effects=True, vmem_limit_bytes=48 * 1024 * 1024
        ),
    )(images, texts, log_temp, bias)
    return image_grad, text_grad, terms[0, 0], terms[0, 1], terms[0, 2]


def solution(mesh, factors=FACTORS):
    in_specs = (P(("row", "col"), None), P(("col", "row"), None), P(), P())
    out_specs = (P(("row", "col"), None), P(("col", "row"), None), P(), P(), P())
    return jax.shard_map(
        functools.partial(on_device, factors),
        mesh=mesh, in_specs=in_specs, out_specs=out_specs, check_vma=False,
    )
```

time: 80 us -> 67 us (0.84)
  Pallas kernels: 74.6 us -> 61.6 us
    pallas_call x1, Pallas kernels: 74.6 us -> 61.6 us  [on_device(): pl.pallas_call(functools.partial(kernel, nx, nzh, nc, ny, nzl, img_to, tx...]
where the time goes in v2:
time: 67 us; the launch traced here: 66.8 us
  Pallas kernels  61.6 us (92%)
  local copies, waits for them, and re-layouts  3.24 us (5%)
  between operations  1.94 us (3%)
    pallas_call x1, Pallas kernels, on_device(): pl.pallas_call(functools.partial(kernel, nx, nzh, nc, ny, nzl, img_to, tx...  61.6 us
    unnamed x6, local copies, waits for them, and re-layouts  2.65 us

profile of v2, /device:TPU:1, one launch (start us, length us, event | category | flops | bytes accessed | tf_op | source)
XLA Modules:
  0.0 66.8 jit_solution(14647440116823754458)
XLA Ops:
  1.9 0.0 copy-start
  1.9 0.7 %copy-done = f32[4,1152]{1,0:T(4,128)S(1)} copy-done((f32[4,1152]{1,0:T(4,128)S(1)}, f32[4,1152]{1,0:T(4,128)}, u32[]{:S(2)}) %copy-start) | copy-done | bytes 18456
  2.6 0.0 copy-start.1
  2.6 0.7 %copy-done.1 = f32[4,1152]{1,0:T(4,128)S(1)} copy-done((f32[4,1152]{1,0:T(4,128)S(1)}, f32[4,1152]{1,0:T(4,128)}, u32[]{:S(2)}) %copy-start.1) | copy-done | bytes 18456
  3.4 61.6 %shard_map.83 = (f32[4,1152]{1,0:T(4,128)S(1)}, f32[4,1152]{1,0:T(4,128)S(1)}, f32[1,128]{1,0:T(1,128)S(1)}) custom-call(f32[4,1152]{1,0:T(4,128)S(1)} %copy-done, f32[4,1152]{1,0:T(4,128)S(1)} %copy-done.1, f32[1]{0:T(128)S(6)} %copy.11.log_temp, f32[1]{0:T(128)S(6)} %copy.12.bias), custom_call_target="tpu_custom_call" | custom-call | tf_op jit(solution)/shard_map/pallas_call | solution.py:229
  65.0 0.6 fusion
  65.6 0.6 copy.13
  66.2 0.6 copy.14
Async XLA Ops:
  1.9 0.7 %copy-start = (f32[4,1152]{1,0:T(4,128)S(1)}, f32[4,1152]{1,0:T(4,128)}, u32[]{:S(2)}) copy-start(f32[4,1152]{1,0:T(4,128)} %images.1) | copy-start | bytes 55300
  2.6 0.7 %copy-start.1 = (f32[4,1152]{1,0:T(4,128)S(1)}, f32[4,1152]{1,0:T(4,128)}, u32[]{:S(2)}) copy-start(f32[4,1152]{1,0:T(4,128)} %texts.1) | copy-start | bytes 55300

commit v3 on v2

--- a/solution.py
+++ b/solution.py
@@ -13,7 +13,8 @@
 
 FACTORS = dict(
     nx=4, nzh=2, nc=2, ny=4, nzl=16,
-    img_to=(9, -8, 8, -7), txt_to=(7, -7, 5, -5, 3, -3, 1, -1),
+    img_steps=(4, -4), img_next=((5, 4), (-4, -3)), txt_steps=(4, -4), txt_next=(1, -1, 3, -3),
+    greet=(4, 3, 1), reach=(13, 12), relay=8,
 )
 
 
@@ -24,16 +25,18 @@
 
 
 def kernel(
-    nx, nzh, nc, ny, nzl, img_to, txt_to,
+    nx, nzh, nc, ny, nzl, img_steps, img_next, txt_steps, txt_next, greet, reach, relay,
     images, texts, log_temp, bias,
     image_grad, text_grad, terms,
-    raw, unit, norm, img_own, txt_own, img_all, txt_all, img_out, txt_out, img_in, txt_in,
+    raw, unit, norm, img_own, txt_own, img_way, txt_way, img_all, txt_all, img_out, txt_out, img_in, txt_in,
     img_zout, txt_zout, img_zin, txt_zin, sc_near, sc_z, load_sem,
-    s_iz, r_iz, s_tz, r_tz, s_ix, r_ix, s_ty, r_ty,
-    s_bx, r_bx, s_by, r_by, s_bi, r_bi, s_bt, r_bt, s_sn, r_sn, s_sz, r_sz,
+    s_iw, r_iw, s_tw, r_tw, s_iz, r_iz, s_tz, r_tz, s_ix, r_ix, s_ty, r_ty,
+    s_bx, r_bx, s_by, r_by, s_bi, r_bi, s_bt, r_bt, s_sn, r_sn, s_sz, r_sz, r_relay,
 ):
     own, width = images.shape
     nz, nxc, nq = nzh * nzl, nx * nc, nx * ny * nc
+    img_to = [a + b for a, after in zip(img_steps, img_next) for b in after]
+    txt_to = [a + b for b in txt_next for a in txt_steps]
     na, nb = len(img_to), len(txt_to)
     row, col = lax.axis_index("row"), lax.axis_index("col")
     x, zh, core = row // (nzh * nc), (row // nc) % nzh, row % nc
@@ -54,7 +57,7 @@
         to = lax.rem(y + k, ny)
         return to, device(x, to, core, z)
 
-    z_steps = sorted({s % nz for a in img_to + txt_to for s in (a, -a)}, key=lambda s: -min(s, nz - s))
+    z_steps = sorted({s % nz for a in greet for s in (a, -a)}, key=lambda s: -min(s, nz - s))
     greeted = [at_z(s) for s in z_steps]
     greeted += [at_y(k)[1] for k in range(1, ny)] + [at_xc(k)[1] for k in range(1, nxc)]
     barrier = pltpu.get_barrier_semaphore()
@@ -89,28 +92,53 @@
     def arrived(slot, sem):
         remote(slot, slot, sem, sem, at_z(1)).wait_recv()
 
-    trips = [(abs(a), 0, i, a) for i, a in enumerate(img_to)] + [(abs(b), 1, i, b) for i, b in enumerate(txt_to)]
-    for _, kind, i, step in sorted(trips, key=lambda t: -t[0]):
-        if kind == 0:
-            send(img_own, img_all.at[xc, i], s_iz.at[i], r_iz.at[i], at_z(step))
-        else:
-            send(txt_own, txt_all.at[y, i], s_tz.at[i], r_tz.at[i], at_z(step))
-    for i in range(nb):
-        arrived(txt_all.at[y, i], r_tz.at[i])
-    for k in range(1, ny):
-        to, dev = at_y(k)
-        send(txt_all.at[y], txt_all.at[y], s_ty.at[to], r_ty.at[y], dev)
-    for i in range(na):
-        arrived(img_all.at[xc, i], r_iz.at[i])
-    for k in range(1, nxc):
-        to, dev = at_xc(k)
-        send(img_all.at[xc], img_all.at[xc], s_ix.at[to], r_ix.at[xc], dev)
-    for k in range(1, ny):
-        to, _ = at_y(k)
-        arrived(txt_all.at[to], r_ty.at[to])
-    for k in range(1, nxc):
-        to, _ = at_xc(k)
-        arrived(img_all.at[to], r_ix.at[to])
+    for i, step in enumerate(img_steps):
+        send(img_own, img_way.at[i], s_iw.at[i], r_iw.at[i], at_z(step))
+    for i, step in enumerate(txt_steps):
+        send(txt_own, txt_way.at[i], s_tw.at[i], r_tw.at[i], at_z(step))
+    for i in range(len(img_steps)):
+        arrived(img_way.at[i], r_iw.at[i])
+    for i in range(len(txt_steps)):
+        arrived(txt_way.at[i], r_tw.at[i])
+    hops = [(way, step) for way, after in enumerate(img_next) for step in after]
+    for i, (way, step) in enumerate(hops):
+        send(img_way.at[way], img_all.at[xc, i], s_iz.at[i], r_iz.at[i], at_z(step))
+    for i, step in reversed(list(enumerate(txt_next))):
+        send(txt_way, txt_all.at[y, i], s_tz.at[i], r_tz.at[i], at_z(step))
+    half = max(1, len(txt_next) // 2)
+    batches = [pl.ds(i, half) for i in range(0, len(txt_next), half)]
+
+    def text_batch(n):
+        for i in range(n * half, n * half + half):
+            arrived(txt_all.at[y, i], r_tz.at[i])
+        for k in range(1, ny):
+            to, dev = at_y(k)
+            block = txt_all.at[y, batches[n]]
+            send(block, block, s_ty.at[n, to], r_ty.at[n, y], dev)
+
+    pairs_of = [pl.ds(0, 2), pl.ds(2, 2)]
+
+    def image_batch(n):
+        for i in (2 * n, 2 * n + 1):
+            arrived(img_all.at[xc, i], r_iz.at[i])
+        for k in range(1, nxc):
+            to, dev = at_xc(k)
+            block = img_all.at[xc, pairs_of[n]]
+            send(block, block, s_ix.at[n, to], r_ix.at[n, xc], dev)
+
+    text_batch(0)
+    image_batch(1)
+    for n in range(1, len(batches)):
+        text_batch(n)
+    image_batch(0)
+    for n, batch in enumerate(batches):
+        for k in range(1, ny):
+            to, _ = at_y(k)
+            arrived(txt_all.at[to, batch], r_ty.at[n, to])
+    for n in (1, 0):
+        for k in range(1, nxc):
+            to, _ = at_xc(k)
+            arrived(img_all.at[to, pairs_of[n]], r_ix.at[n, to])
 
     n_img, n_txt = nxc * na * own, ny * nb * own
     img = img_all[...].astype(F32).reshape(n_img, width).astype(BF16)
@@ -151,40 +179,56 @@
         to = lax.rem(q + k, nq)
         dev = device(to // (ny * nc), (to // nc) % ny, lax.rem(to, nc), z)
         remote(sc_near.at[q], sc_near.at[q], s_sn, r_sn, dev).start()
-
     low = dlogit.astype(BF16)
-    txt_part = jnp.dot(low, img, preferred_element_type=F32)
-    txt_out[...] = txt_part.reshape(ny, nb, own, width).astype(BF16)
-    for k in range(1, ny):
-        to, dev = at_y(k)
-        send(txt_out.at[to], txt_in.at[y], s_by.at[to], r_by.at[y], dev)
     img_part = lax.dot_general(low, txt, (((0,), (0,)), ((), ())), preferred_element_type=F32)
     img_out[...] = img_part.reshape(nxc, na, own, width).astype(BF16)
-    for k in range(1, nxc):
-        to, dev = at_xc(k)
-        send(img_out.at[to], img_in.at[xc], s_bx.at[to], r_bx.at[xc], dev)
+    for n, pair in enumerate(pairs_of):
+        for k in range(1, nxc):
+            to, dev = at_xc(k)
+            send(img_out.at[to, pair], img_in.at[xc, pair], s_bx.at[n, to], r_bx.at[n, xc], dev)
+    txt_part = jnp.dot(low, img, preferred_element_type=F32)
+    txt_out[...] = txt_part.reshape(ny, nb // 2, 2, own, width).astype(BF16)
+    for n, batch in reversed(list(enumerate(batches))):
+        for k in range(1, ny):
+            to, dev = at_y(k)
+            send(txt_out.at[to, batch], txt_in.at[y, batch], s_by.at[n, to], r_by.at[n, y], dev)
 
     remote(sc_near.at[pl.ds(0, nq - 1)], sc_near.at[pl.ds(0, nq - 1)], s_sn, r_sn, at_z(1)).wait_recv()
     sc_z[z] = jnp.sum(sc_near[...], axis=0)
-    for k in sorted(range(1, nz), key=lambda s: -min(s, nz - s)):
-        remote(sc_z.at[z], sc_z.at[z], s_sz, r_sz, at_z(k)).start()
-
-    acc = txt_out[y].astype(F32)
-    for k in range(1, ny):
-        to, _ = at_y(k)
-        arrived(txt_in.at[to], r_by.at[to])
-        acc += txt_in[to].astype(F32)
-    txt_zout[...] = acc.astype(BF16)
-    for i, b in enumerate(txt_to):
-        send(txt_zout.at[i], txt_zin.at[i], s_bt.at[i], r_bt.at[i], at_z(-b))
-    acc = img_out[xc].astype(F32)
-    for k in range(1, nxc):
-        to, _ = at_xc(k)
-        arrived(img_in.at[to], r_bx.at[to])
-        acc += img_in[to].astype(F32)
-    img_zout[...] = acc.astype(BF16)
-    for i, a in enumerate(img_to):
-        send(img_zout.at[i], img_zin.at[i], s_bi.at[i], r_bi.at[i], at_z(-a))
+    offsets = sorted((s for s in range(-nz // 2 + 1, nz // 2 + 1)), key=lambda s: -abs(s))
+    straight = [s for s in offsets if s != 0 and -reach[0] <= s <= reach[1]]
+    relayed = [s for s in offsets if s not in straight and s != 0]
+    legs = [(s - relay, relay) if s > 0 else (s + relay, -relay) for s in relayed]
+    first = [leg for leg, _ in legs]
+    for s in straight:
+        sem = r_relay.at[first.index(s)] if s in first else r_sz
+        remote(sc_z.at[z], sc_z.at[z], s_sz, sem, at_z(s)).start()
+
+    for n, pair in enumerate(pairs_of):
+        acc = img_out[xc, pair].astype(F32)
+        for k in range(1, nxc):
+            to, _ = at_xc(k)
+            arrived(img_in.at[to, pair], r_bx.at[n, to])
+            acc += img_in[to, pair].astype(F32)
+        img_zout[pair] = acc.astype(BF16)
+        for i in (2 * n, 2 * n + 1):
+            send(img_zout.at[i], img_zin.at[i], s_bi.at[i], r_bi.at[i], at_z(-img_to[i]))
+    for n, batch in reversed(list(enumerate(batches))):
+        acc = txt_out[y, batch].astype(F32)
+        for k in range(1, ny):
+            to, _ = at_y(k)
+            arrived(txt_in.at[to, batch], r_by.at[n, to])
+            acc += txt_in[to, batch].astype(F32)
+        txt_zout[batch] = acc.astype(BF16)
+        for i in range(n * half, n * half + half):
+            for j in range(2):
+                at = i * 2 + j
+                send(txt_zout.at[i, j], txt_zin.at[at], s_bt.at[at], r_bt.at[at], at_z(-txt_to[at]))
+
+    for n, (leg, on) in enumerate(legs):
+        slot = sc_z.at[lax.rem(z - leg + nz, nz)]
+        arrived(slot, r_relay.at[n])
+        remote(slot, slot, s_sz, r_sz, at_z(on)).start()
 
     def finish(at, gathered, sem, out):
         for i in range(gathered.shape[0]):
@@ -203,6 +247,7 @@
     remote(rest, rest, s_sn, r_sn, at_z(1)).wait_send()
     rest = sc_z.at[pl.ds(0, nz - 1)]
     remote(rest, rest, s_sz, r_sz, at_z(1)).wait_send()
+    rest = sc_z.at[pl.ds(0, nz - 1 - len(legs))]
     remote(rest, rest, s_sz, r_sz, at_z(1)).wait_recv()
     pairs = float(rows * cols * own)
     scale = 1.0 / (pairs * pairs)
@@ -211,10 +256,9 @@
 
 
 def on_device(factors, images, texts, log_temp, bias):
-    nx, nzh, nc, ny, nzl, img_to, txt_to = (
-        factors[k] for k in ("nx", "nzh", "nc", "ny", "nzl", "img_to", "txt_to")
-    )
-    nxc, na, nb = nx * nc, len(img_to), len(txt_to)
+    nx, nzh, nc, ny, nzl = (factors[k] for k in ("nx", "nzh", "nc", "ny", "nzl"))
+    nxc, na, nn = nx * nc, sum(len(n) for n in factors["img_next"]), len(factors["txt_next"])
+    nb, nw = 2 * nn, max(1, nn // (nn // 2 or 1))
     own, width = images.shape
     vmem = pl.BlockSpec(memory_space=pltpu.VMEM)
     smem = pl.BlockSpec(memory_space=pltpu.SMEM)
@@ -224,10 +268,10 @@
         return pltpu.VMEM(lead + (own, width), BF16)
 
     def sems(*counts):
-        return [pltpu.SemaphoreType.DMA((c,)) for c in counts for _ in range(2)]
+        return [pltpu.SemaphoreType.DMA(c) for c in counts for _ in range(2)]
 
     image_grad, text_grad, terms = pl.pallas_call(
-        functools.partial(kernel, nx, nzh, nc, ny, nzl, img_to, txt_to),
+        functools.partial(kernel, *factors.values()),
         out_shape=(
             jax.ShapeDtypeStruct((own, width), F32),
             jax.ShapeDtypeStruct((own, width), F32),
@@ -239,16 +283,18 @@
             pltpu.VMEM((2, own, width), F32),
             pltpu.VMEM((2, own, width), F32),
             pltpu.VMEM((2, own, 1), F32),
-            low(), low(),
-            low(nxc, na), low(ny, nb),
-            low(nxc, na), low(ny, nb), low(nxc, na), low(ny, nb),
-            low(na), low(nb), low(na), low(nb),
+            low(), low(), low(2), low(2),
+            low(nxc, na), low(ny, nn, 2),
+            low(nxc, na), low(ny, nn, 2), low(nxc, na), low(ny, nn, 2),
+            low(na), low(nn, 2), low(na), low(nb),
             pltpu.VMEM((nx * ny * nc, 1, 128), F32),
             pltpu.VMEM((nzh * nzl, 1, 128), F32),
             pltpu.SemaphoreType.DMA((2,)),
-        ] + sems(na, nb, nxc, ny, nxc, ny, na, nb) + [pltpu.SemaphoreType.DMA] * 4,
+        ] + sems(
+            (2,), (2,), (na,), (nn,), (2, nxc), (nw, ny), (2, nxc), (nw, ny), (na,), (nb,), (), ()
+        ) + [pltpu.SemaphoreType.DMA((8,))],
         compiler_params=pltpu.CompilerParams(
-            collective_id=0, has_side_effects=True, vmem_limit_bytes=48 * 1024 * 1024
+            collective_id=0, has_side_effects=True
         ),
     )(images, texts, log_temp, bias)
     return image_grad, text_grad, terms[0, 0], terms[0, 1], terms[0, 2]

time: 67 us -> 65.7 us (0.981)
  the two profiles are of different devices: /device:TPU:1 before, /device:TPU:6 now
where the time goes in v3:
time: 65.7 us; the launch traced here: 65.4 us
  Pallas kernels  60.8 us (93%)
  local copies, waits for them, and re-layouts  2.64 us (4%)
  between operations  1.94 us (3%)
    pallas_call x1, Pallas kernels, on_device(): pl.pallas_call(functools.partial(kernel, *factors.values()), out_shape=(j...  60.8 us
    unnamed x6, local copies, waits for them, and re-layouts  1.34 us

profile of v3, /device:TPU:6, one launch (start us, length us, event | category | flops | bytes accessed | tf_op | source)
XLA Modules:
  0.0 65.4 jit_solution(15601861558040886119)
XLA Ops:
  1.9 60.8 %shard_map.83 = (f32[4,1152]{1,0:T(4,128)}, f32[4,1152]{1,0:T(4,128)}, f32[1,128]{1,0:T(1,128)}) custom-call(f32[4,1152]{1,0:T(4,128)} %images.1, f32[4,1152]{1,0:T(4,128)} %texts.1, f32[1]{0:T(128)S(6)} %copy.11.log_temp, f32[1]{0:T(128)S(6)} %copy.12.bias), custom_call_target="tpu_custom_call" | custom-call | tf_op jit(solution)/shard_map/pallas_call | solution.py:273
  62.7 0.0 copy-start.1
  62.8 1.3 %fusion = (f32[1,1]{1,0:T(1,128)}, f32[1,1]{1,0:T(1,128)}, f32[1,1]{1,0:T(1,128)}) fusion(f32[1,128]{1,0:T(1,128)} %get-tuple-element.10), kind=kLoop, calls=%fused_computation | loop fusion | bytes 24 | tf_op jit(solution)/shard_map/slice | solution.py:300
  64.1 0.0 copy-done.1
  64.1 0.0 copy-start
  64.1 0.6 copy.13
  64.7 0.1 copy-done
  64.8 0.6 copy.14
Async XLA Ops:
  62.7 1.3 %copy-start.1 = (f32[4,1152]{1,0:T(4,128)S(1)}, f32[4,1152]{1,0:T(4,128)}, u32[]{:S(2)}) copy-start(f32[4,1152]{1,0:T(4,128)} %get-tuple-element.19) | copy-start | bytes 55300
  64.1 0.7 %copy-start = (f32[4,1152]{1,0:T(4,128)S(1)}, f32[4,1152]{1,0:T(4,128)}, u32[]{:S(2)}) copy-start(f32[4,1152]{1,0:T(4,128)} %get-tuple-element.20) | copy-start | bytes 55300

commit v4 on v3

--- a/solution.py
+++ b/solution.py
@@ -14,7 +14,7 @@
 FACTORS = dict(
     nx=4, nzh=2, nc=2, ny=4, nzl=16,
     img_steps=(4, -4), img_next=((5, 4), (-4, -3)), txt_steps=(4, -4), txt_next=(1, -1, 3, -3),
-    greet=(4, 3, 1), reach=(13, 12), relay=8,
+    greet=(4, 3, 2, 1), far=8,
 )
 
 
@@ -25,13 +25,13 @@
 
 
 def kernel(
-    nx, nzh, nc, ny, nzl, img_steps, img_next, txt_steps, txt_next, greet, reach, relay,
+    nx, nzh, nc, ny, nzl, img_steps, img_next, txt_steps, txt_next, greet, far,
     images, texts, log_temp, bias,
     image_grad, text_grad, terms,
     raw, unit, norm, img_own, txt_own, img_way, txt_way, img_all, txt_all, img_out, txt_out, img_in, txt_in,
     img_zout, txt_zout, img_zin, txt_zin, sc_near, sc_z, load_sem,
     s_iw, r_iw, s_tw, r_tw, s_iz, r_iz, s_tz, r_tz, s_ix, r_ix, s_ty, r_ty,
-    s_bx, r_bx, s_by, r_by, s_bi, r_bi, s_bt, r_bt, s_sn, r_sn, s_sz, r_sz, r_relay,
+    s_bx, r_bx, s_by, r_by, s_bi, r_bi, s_bt, r_bt, s_sn, r_sn, s_sz, r_sz, ready,
 ):
     own, width = images.shape
     nz, nxc, nq = nzh * nzl, nx * nc, nx * ny * nc
@@ -100,6 +100,8 @@
         arrived(img_way.at[i], r_iw.at[i])
     for i in range(len(txt_steps)):
         arrived(txt_way.at[i], r_tw.at[i])
+    for step in (far, -far):
+        pl.semaphore_signal(ready, inc=1, device_id=at_z(step), device_id_type=MESH)
     hops = [(way, step) for way, after in enumerate(img_next) for step in after]
     for i, (way, step) in enumerate(hops):
         send(img_way.at[way], img_all.at[xc, i], s_iz.at[i], r_iz.at[i], at_z(step))
@@ -172,13 +174,12 @@
         return jnp.sum(jnp.sum(v, axis=0, keepdims=True), axis=1, keepdims=True)
 
     lane = lax.broadcasted_iota(jnp.int32, (1, 128), 1)
-    sc_near[q] = jnp.where(
+    sc_z[z] = jnp.where(
         lane == 0, total(loss), jnp.where(lane == 1, total(dlogit * scores), total(dlogit))
     )
-    for k in range(1, nq):
-        to = lax.rem(q + k, nq)
-        dev = device(to // (ny * nc), (to // nc) % ny, lax.rem(to, nc), z)
-        remote(sc_near.at[q], sc_near.at[q], s_sn, r_sn, dev).start()
+    pl.semaphore_wait(ready, 2)
+    for step in sorted(range(1, nz), key=lambda s: -min(s, nz - s)):
+        remote(sc_z.at[z], sc_z.at[z], s_sz, r_sz, at_z(step)).start()
     low = dlogit.astype(BF16)
     img_part = lax.dot_general(low, txt, (((0,), (0,)), ((), ())), preferred_element_type=F32)
     img_out[...] = img_part.reshape(nxc, na, own, width).astype(BF16)
@@ -192,17 +193,6 @@
         for k in range(1, ny):
             to, dev = at_y(k)
             send(txt_out.at[to, batch], txt_in.at[y, batch], s_by.at[n, to], r_by.at[n, y], dev)
-
-    remote(sc_near.at[pl.ds(0, nq - 1)], sc_near.at[pl.ds(0, nq - 1)], s_sn, r_sn, at_z(1)).wait_recv()
-    sc_z[z] = jnp.sum(sc_near[...], axis=0)
-    offsets = sorted((s for s in range(-nz // 2 + 1, nz // 2 + 1)), key=lambda s: -abs(s))
-    straight = [s for s in offsets if s != 0 and -reach[0] <= s <= reach[1]]
-    relayed = [s for s in offsets if s not in straight and s != 0]
-    legs = [(s - relay, relay) if s > 0 else (s + relay, -relay) for s in relayed]
-    first = [leg for leg, _ in legs]
-    for s in straight:
-        sem = r_relay.at[first.index(s)] if s in first else r_sz
-        remote(sc_z.at[z], sc_z.at[z], s_sz, sem, at_z(s)).start()
 
     for n, pair in enumerate(pairs_of):
         acc = img_out[xc, pair].astype(F32)
@@ -225,10 +215,13 @@
                 at = i * 2 + j
                 send(txt_zout.at[i, j], txt_zin.at[at], s_bt.at[at], r_bt.at[at], at_z(-txt_to[at]))
 
-    for n, (leg, on) in enumerate(legs):
-        slot = sc_z.at[lax.rem(z - leg + nz, nz)]
-        arrived(slot, r_relay.at[n])
-        remote(slot, slot, s_sz, r_sz, at_z(on)).start()
+    others = sc_z.at[pl.ds(0, nz - 1)]
+    remote(others, others, s_sz, r_sz, at_z(1)).wait_recv()
+    sc_near[q] = jnp.sum(sc_z[...], axis=0)
+    for k in range(1, nq):
+        to = lax.rem(q + k, nq)
+        dev = device(to // (ny * nc), (to // nc) % ny, lax.rem(to, nc), z)
+        remote(sc_near.at[q], sc_near.at[q], s_sn, r_sn, dev).start()
 
     def finish(at, gathered, sem, out):
         for i in range(gathered.shape[0]):
@@ -243,15 +236,13 @@
 
     for copy in pending:
         copy.wait_send()
+    remote(others, others, s_sz, r_sz, at_z(1)).wait_send()
     rest = sc_near.at[pl.ds(0, nq - 1)]
     remote(rest, rest, s_sn, r_sn, at_z(1)).wait_send()
-    rest = sc_z.at[pl.ds(0, nz - 1)]
-    remote(rest, rest, s_sz, r_sz, at_z(1)).wait_send()
-    rest = sc_z.at[pl.ds(0, nz - 1 - len(legs))]
-    remote(rest, rest, s_sz, r_sz, at_z(1)).wait_recv()
+    remote(rest, rest, s_sn, r_sn, at_z(1)).wait_recv()
     pairs = float(rows * cols * own)
     scale = 1.0 / (pairs * pairs)
-    result = jnp.sum(sc_z[...], axis=0) * scale
+    result = jnp.sum(sc_near[...], axis=0) * scale
     terms[...] = jnp.where(lane == 1, temp, 1.0) * result
 
 
@@ -292,7 +283,7 @@
             pltpu.SemaphoreType.DMA((2,)),
         ] + sems(
             (2,), (2,), (na,), (nn,), (2, nxc), (nw, ny), (2, nxc), (nw, ny), (na,), (nb,), (), ()
-        ) + [pltpu.SemaphoreType.DMA((8,))],
+        ) + [pltpu.SemaphoreType.REGULAR],
         compiler_params=pltpu.CompilerParams(
             collective_id=0, has_side_effects=True
         ),

time: 65.7 us -> 61.9 us (0.942)
  the two profiles are of different devices: /device:TPU:6 before, /device:TPU:1 now
where the time goes in v4:
time: 61.9 us; the launch traced here: 61.6 us
  Pallas kernels  57 us (92%)
  local copies, waits for them, and re-layouts  2.64 us (4%)
  between operations  1.94 us (3%)
    pallas_call x1, Pallas kernels, on_device(): pl.pallas_call(functools.partial(kernel, *factors.values()), out_shape=(j...  57 us
    unnamed x6, local copies, waits for them, and re-layouts  1.34 us
    slice x1, local copies, waits for them, and re-layouts, on_device(): return (image_grad, text_grad, terms[0, 0], terms[0, 1], terms[0, 2])  1.3 us

profile of v4, /device:TPU:1, one launch (start us, length us, event | category | flops | bytes accessed | tf_op | source)
XLA Modules:
  0.0 61.6 jit_solution(9706390887832886884)
XLA Ops:
  1.9 57.0 %shard_map.83 = (f32[4,1152]{1,0:T(4,128)}, f32[4,1152]{1,0:T(4,128)}, f32[1,128]{1,0:T(1,128)}) custom-call(f32[4,1152]{1,0:T(4,128)} %images.1, f32[4,1152]{1,0:T(4,128)} %texts.1, f32[1]{0:T(128)S(6)} %copy.11.log_temp, f32[1]{0:T(128)S(6)} %copy.12.bias), custom_call_target="tpu_custom_call" | custom-call | tf_op jit(solution)/shard_map/pallas_call | solution.py:264
  58.9 0.0 copy-start.1
  58.9 1.3 %fusion = (f32[1,1]{1,0:T(1,128)}, f32[1,1]{1,0:T(1,128)}, f32[1,1]{1,0:T(1,128)}) fusion(f32[1,128]{1,0:T(1,128)} %get-tuple-element.10), kind=kLoop, calls=%fused_computation | loop fusion | bytes 24 | tf_op jit(solution)/shard_map/slice | solution.py:291
  60.2 0.0 copy-done.1
  60.2 0.0 copy-start
  60.3 0.6 copy.13
  60.9 0.1 copy-done
  61.0 0.6 copy.14
Async XLA Ops:
  58.9 1.3 %copy-start.1 = (f32[4,1152]{1,0:T(4,128)S(1)}, f32[4,1152]{1,0:T(4,128)}, u32[]{:S(2)}) copy-start(f32[4,1152]{1,0:T(4,128)} %get-tuple-element.19) | copy-start | bytes 55300
  60.2 0.7 %copy-start = (f32[4,1152]{1,0:T(4,128)S(1)}, f32[4,1152]{1,0:T(4,128)}, u32[]{:S(2)}) copy-start(f32[4,1152]{1,0:T(4,128)} %get-tuple-element.20) | copy-start | bytes 55300

commit v5 on v4

--- a/solution.py
+++ b/solution.py
@@ -27,9 +27,9 @@
 def kernel(
     nx, nzh, nc, ny, nzl, img_steps, img_next, txt_steps, txt_next, greet, far,
     images, texts, log_temp, bias,
-    image_grad, text_grad, terms,
+    grads, terms,
     raw, unit, norm, img_own, txt_own, img_way, txt_way, img_all, txt_all, img_out, txt_out, img_in, txt_in,
-    img_zout, txt_zout, img_zin, txt_zin, sc_near, sc_z, load_sem,
+    img_zout, txt_zout, img_zin, txt_zin, sc_near, sc_z, held, load_sem,
     s_iw, r_iw, s_tw, r_tw, s_iz, r_iz, s_tz, r_tz, s_ix, r_ix, s_ty, r_ty,
     s_bx, r_bx, s_by, r_by, s_bi, r_bi, s_bt, r_bt, s_sn, r_sn, s_sz, r_sz, ready,
 ):
@@ -65,13 +65,13 @@
         pl.semaphore_signal(barrier, inc=1, device_id=dev, device_id_type=MESH)
 
     loads = [
-        pltpu.make_async_copy(ref, raw.at[at], load_sem.at[at])
-        for at, ref in enumerate((images, texts))
+        pltpu.make_async_copy(ref, to, load_sem.at[at])
+        for at, (ref, to) in enumerate(
+            ((images, raw.at[0]), (texts, raw.at[1]), (log_temp, held.at[0]), (bias, held.at[1]))
+        )
     ]
     for load in loads:
         load.start()
-    temp = jnp.exp(jnp.full((1, 1), log_temp[0], F32))
-    offset = bias[0]
     for at, slot in ((0, img_own), (1, txt_own)):
         loads[at].wait()
         v = raw[at]
@@ -80,6 +80,10 @@
         norm[at] = n
         unit[at] = u
         slot[...] = u.astype(BF16)
+    for load in loads[2:]:
+        load.wait()
+    temp = jnp.exp(jnp.full((1, 1), held[0, 0], F32))
+    offset = held[1, 0]
     pl.semaphore_wait(barrier, len(greeted))
 
     pending = []
@@ -194,7 +198,8 @@
             to, dev = at_y(k)
             send(txt_out.at[to, batch], txt_in.at[y, batch], s_by.at[n, to], r_by.at[n, y], dev)
 
-    for n, pair in enumerate(pairs_of):
+    def return_images(n):
+        pair = pairs_of[n]
         acc = img_out[xc, pair].astype(F32)
         for k in range(1, nxc):
             to, _ = at_xc(k)
@@ -203,7 +208,9 @@
         img_zout[pair] = acc.astype(BF16)
         for i in (2 * n, 2 * n + 1):
             send(img_zout.at[i], img_zin.at[i], s_bi.at[i], r_bi.at[i], at_z(-img_to[i]))
-    for n, batch in reversed(list(enumerate(batches))):
+
+    def return_texts(n):
+        batch = batches[n]
         acc = txt_out[y, batch].astype(F32)
         for k in range(1, ny):
             to, _ = at_y(k)
@@ -215,6 +222,12 @@
                 at = i * 2 + j
                 send(txt_zout.at[i, j], txt_zin.at[at], s_bt.at[at], r_bt.at[at], at_z(-txt_to[at]))
 
+    return_images(0)
+    return_texts(len(batches) - 1)
+    return_images(1)
+    for n in range(len(batches) - 1):
+        return_texts(n)
+
     others = sc_z.at[pl.ds(0, nz - 1)]
     remote(others, others, s_sz, r_sz, at_z(1)).wait_recv()
     sc_near[q] = jnp.sum(sc_z[...], axis=0)
@@ -223,16 +236,16 @@
         dev = device(to // (ny * nc), (to // nc) % ny, lax.rem(to, nc), z)
         remote(sc_near.at[q], sc_near.at[q], s_sn, r_sn, dev).start()
 
-    def finish(at, gathered, sem, out):
+    def finish(at, gathered, sem):
         for i in range(gathered.shape[0]):
             arrived(gathered.at[i], sem.at[i])
         g = temp * jnp.sum(gathered[...].astype(F32), axis=0)
         u = unit[at]
         along = jnp.sum(u * g, axis=-1, keepdims=True)
-        out[...] = (g - u * along) / norm[at]
-
-    finish(1, txt_zin, r_bt, text_grad)
-    finish(0, img_zin, r_bi, image_grad)
+        grads[at] = (g - u * along) / norm[at]
+
+    finish(1, txt_zin, r_bt)
+    finish(0, img_zin, r_bi)
 
     for copy in pending:
         copy.wait_send()
@@ -251,9 +264,9 @@
     nxc, na, nn = nx * nc, sum(len(n) for n in factors["img_next"]), len(factors["txt_next"])
     nb, nw = 2 * nn, max(1, nn // (nn // 2 or 1))
     own, width = images.shape
+    n_pairs = (nxc * na * own) * (ny * nb * own)
     vmem = pl.BlockSpec(memory_space=pltpu.VMEM)
-    smem = pl.BlockSpec(memory_space=pltpu.SMEM)
-    hbm = pl.BlockSpec(memory_space=pl.ANY)
+    hbm = pl.BlockSpec(memory_space=pltpu.HBM)
 
     def low(*lead):
         return pltpu.VMEM(lead + (own, width), BF16)
@@ -261,15 +274,14 @@
     def sems(*counts):
         return [pltpu.SemaphoreType.DMA(c) for c in counts for _ in range(2)]
 
-    image_grad, text_grad, terms = pl.pallas_call(
+    grads, terms = pl.pallas_call(
         functools.partial(kernel, *factors.values()),
         out_shape=(
-            jax.ShapeDtypeStruct((own, width), F32),
-            jax.ShapeDtypeStruct((own, width), F32),
+            jax.ShapeDtypeStruct((2, own, width), F32),
             jax.ShapeDtypeStruct((1, 128), F32),
         ),
-        in_specs=[hbm, hbm, smem, smem],
-        out_specs=(vmem, vmem, vmem),
+        in_specs=[hbm] * 4,
+        out_specs=(vmem, vmem),
         scratch_shapes=[
             pltpu.VMEM((2, own, width), F32),
             pltpu.VMEM((2, own, width), F32),
@@ -280,15 +292,17 @@
             low(na), low(nn, 2), low(na), low(nb),
             pltpu.VMEM((nx * ny * nc, 1, 128), F32),
             pltpu.VMEM((nzh * nzl, 1, 128), F32),
-            pltpu.SemaphoreType.DMA((2,)),
+            pltpu.SMEM((2, 1), F32),
+            pltpu.SemaphoreType.DMA((4,)),
         ] + sems(
             (2,), (2,), (na,), (nn,), (2, nxc), (nw, ny), (2, nxc), (nw, ny), (na,), (nb,), (), ()
         ) + [pltpu.SemaphoreType.REGULAR],
+        cost_estimate=pl.CostEstimate(flops=6 * n_pairs * width, bytes_accessed=4 * own * width * 4, transcendentals=2 * n_pairs),
         compiler_params=pltpu.CompilerParams(
-            collective_id=0, has_side_effects=True
+            collective_id=0, has_side_effects=True, vmem_limit_bytes=32 * 1024 * 1024
         ),
     )(images, texts, log_temp, bias)
-    return image_grad, text_grad, terms[0, 0], terms[0, 1], terms[0, 2]
+    return grads[0], grads[1], terms[0, 0], terms[0, 1], terms[0, 2]
 
 
 def solution(mesh, factors=FACTORS):

time: 61.9 us -> 61.3 us (level)
    slice x1, local copies, waits for them, and re-layouts: 1.3 us -> 0.59 us  [on_device(): return (grads[0], grads[1], terms[0, 0], terms[0, 1], terms[0, 2])]
    unnamed x6 -> x4, local copies, waits for them, and re-layouts: 1.34 us -> 1.44 us
where the time goes in v5:
time: 61.3 us; the launch traced here: 61.1 us
  Pallas kernels  56.5 us (92%)
  local copies, waits for them, and re-layouts  2.64 us (4%)
  between operations  1.94 us (3%)
    pallas_call x1, Pallas kernels, on_device(): pl.pallas_call(functools.partial(kernel, *factors.values()), out_shape=(j...  56.5 us
    unnamed x4, local copies, waits for them, and re-layouts  1.44 us

profile of v5, /device:TPU:1, one launch (start us, length us, event | category | flops | bytes accessed | tf_op | source)
XLA Modules:
  0.0 61.1 jit_solution(1801680009113762739)
XLA Ops:
  1.9 0.0 copy-start
  1.9 0.7 %copy-done = f32[4,1152]{1,0:T(4,128)S(1)} copy-done((f32[4,1152]{1,0:T(4,128)S(1)}, f32[4,1152]{1,0:T(4,128)}, u32[]{:S(2)}) %copy-start) | copy-done | bytes 18456
  2.6 0.0 copy-start.1
  2.6 0.7 %copy-done.1 = f32[4,1152]{1,0:T(4,128)S(1)} copy-done((f32[4,1152]{1,0:T(4,128)S(1)}, f32[4,1152]{1,0:T(4,128)}, u32[]{:S(2)}) %copy-start.1) | copy-done | bytes 18456
  3.4 56.5 %shard_map.83 = (f32[2,4,1152]{2,1,0:T(4,128)S(1)}, f32[1,128]{1,0:T(1,128)S(1)}) custom-call(f32[4,1152]{1,0:T(4,128)S(1)} %copy-done, f32[4,1152]{1,0:T(4,128)S(1)} %copy-done.1, f32[1]{0:T(128)S(6)} %copy.9.log_temp, f32[1]{0:T(128)S(6)} %copy.10.bias), custom_call_target="tpu_custom_call" | custom-call | flops 113246208 | bytes 73728 | tf_op jit(solution)/shard_map/pallas_call | solution.py:277
  59.9 0.6 %slice_bitcast_fusion = (f32[4,1152]{1,0:T(4,128)}, f32[4,1152]{1,0:T(4,128)}) fusion(f32[2,4,1152]{2,1,0:T(4,128)S(1)} %get-tuple-element.7), kind=kLoop, calls=%fused_computation | loop fusion | bytes 73728 | tf_op jit(solution)/shard_map/squeeze | solution.py:305
  60.5 0.6 fusion
Async XLA Ops:
  1.9 0.7 %copy-start = (f32[4,1152]{1,0:T(4,128)S(1)}, f32[4,1152]{1,0:T(4,128)}, u32[]{:S(2)}) copy-start(f32[4,1152]{1,0:T(4,128)} %images.1) | copy-start | bytes 55300
  2.6 0.7 %copy-start.1 = (f32[4,1152]{1,0:T(4,128)S(1)}, f32[4,1152]{1,0:T(4,128)}, u32[]{:S(2)}) copy-start(f32[4,1152]{1,0:T(4,128)} %texts.1) | copy-start | bytes 55300

commit v6 on v5

--- a/solution.py
+++ b/solution.py
@@ -257,6 +257,13 @@
     scale = 1.0 / (pairs * pairs)
     result = jnp.sum(sc_near[...], axis=0) * scale
     terms[...] = jnp.where(lane == 1, temp, 1.0) * result
+
+
+def write_out(grads, terms, image_grad, text_grad, loss, slope, shift):
+    image_grad[...] = grads[0]
+    text_grad[...] = grads[1]
+    for i, out in enumerate((loss, slope, shift)):
+        out[...] = terms[:, i : i + 1]
 
 
 def on_device(factors, images, texts, log_temp, bias):
@@ -302,7 +309,16 @@
             collective_id=0, has_side_effects=True, vmem_limit_bytes=32 * 1024 * 1024
         ),
     )(images, texts, log_temp, bias)
-    return grads[0], grads[1], terms[0, 0], terms[0, 1], terms[0, 2]
+    one = jax.ShapeDtypeStruct((1, 1), F32)
+    block = jax.ShapeDtypeStruct((own, width), F32)
+    image_grad, text_grad, loss, slope, shift = pl.pallas_call(
+        write_out,
+        out_shape=(block, block, one, one, one),
+        in_specs=[vmem] * 2,
+        out_specs=(vmem,) * 5,
+        compiler_params=pltpu.CompilerParams(vmem_limit_bytes=32 * 1024 * 1024),
+    )(grads, terms)
+    return image_grad, text_grad, loss[0, 0], slope[0, 0], shift[0, 0]
 
 
 def solution(mesh, factors=FACTORS):

time: 61.3 us -> 60.8 us (level)
  local copies, waits for them, and re-layouts: 2.64 us -> 1.44 us
    pallas_call x0 -> x1, Pallas kernels: none -> 0.62 us  [on_device(): pl.pallas_call(write_out, out_shape=(block, block, one, one, one), in_spe...]
    squeeze x1 -> x0, local copies, waits for them, and re-layouts: 0.62 us -> none  [on_device(): return (grads[0], grads[1], terms[0, 0], terms[0, 1], terms[0, 2])]
where the time goes in v6:
time: 60.8 us; the launch traced here: 60.5 us
  Pallas kernels  57.1 us (94%)
  between operations  1.94 us (3%)
  local copies, waits for them, and re-layouts  1.44 us (2%)
    pallas_call x1, Pallas kernels, on_device(): pl.pallas_call(functools.partial(kernel, *factors.values()), out_shape=(j...  56.5 us
    unnamed x4, local copies, waits for them, and re-layouts  1.44 us

profile of v6, /device:TPU:1, one launch (start us, length us, event | category | flops | bytes accessed | tf_op | source)
XLA Modules:
  0.0 60.5 jit_solution(12456870585955365613)
XLA Ops:
  1.9 0.0 copy-start
  1.9 0.7 %copy-done = f32[4,1152]{1,0:T(4,128)S(1)} copy-done((f32[4,1152]{1,0:T(4,128)S(1)}, f32[4,1152]{1,0:T(4,128)}, u32[]{:S(2)}) %copy-start) | copy-done | bytes 18456
  2.6 0.0 copy-start.1
  2.6 0.7 %copy-done.1 = f32[4,1152]{1,0:T(4,128)S(1)} copy-done((f32[4,1152]{1,0:T(4,128)S(1)}, f32[4,1152]{1,0:T(4,128)}, u32[]{:S(2)}) %copy-start.1) | copy-done | bytes 18456
  3.4 56.5 %shard_map.83 = (f32[2,4,1152]{2,1,0:T(4,128)S(1)}, f32[1,128]{1,0:T(1,128)S(1)}) custom-call(f32[4,1152]{1,0:T(4,128)S(1)} %copy-done, f32[4,1152]{1,0:T(4,128)S(1)} %copy-done.1, f32[1]{0:T(128)S(6)} %copy.9.log_temp, f32[1]{0:T(128)S(6)} %copy.10.bias), custom_call_target="tpu_custom_call" | custom-call | flops 113246208 | bytes 73728 | tf_op jit(solution)/shard_map/pallas_call | solution.py:284
  59.9 0.6 %shard_map.84 = (f32[4,1152]{1,0:T(4,128)}, f32[4,1152]{1,0:T(4,128)}, f32[1,1]{1,0:T(1,128)}, f32[1,1]{1,0:T(1,128)}, f32[1,1]{1,0:T(1,128)}) custom-call(f32[2,4,1152]{2,1,0:T(4,128)S(1)} %get-tuple-element.12.grads, f32[1,128]{1,0:T(1,128)S(1)} %get-tuple-element.13.terms), custom_call_target="tpu_custom_call" | custom-call | tf_op jit(solution)/shard_map/pallas_call | solution.py:314
Async XLA Ops:
  1.9 0.7 %copy-start = (f32[4,1152]{1,0:T(4,128)S(1)}, f32[4,1152]{1,0:T(4,128)}, u32[]{:S(2)}) copy-start(f32[4,1152]{1,0:T(4,128)} %images.1) | copy-start | bytes 55300
  2.6 0.7 %copy-start.1 = (f32[4,1152]{1,0:T(4,128)S(1)}, f32[4,1152]{1,0:T(4,128)}, u32[]{:S(2)}) copy-start(f32[4,1152]{1,0:T(4,128)} %texts.1) | copy-start | bytes 55300

commit v7 on v6

--- a/solution.py
+++ b/solution.py
@@ -27,9 +27,9 @@
 def kernel(
     nx, nzh, nc, ny, nzl, img_steps, img_next, txt_steps, txt_next, greet, far,
     images, texts, log_temp, bias,
-    grads, terms,
+    grads_out, terms,
     raw, unit, norm, img_own, txt_own, img_way, txt_way, img_all, txt_all, img_out, txt_out, img_in, txt_in,
-    img_zout, txt_zout, img_zin, txt_zin, sc_near, sc_z, held, load_sem,
+    img_zout, txt_zout, img_zin, txt_zin, sc_near, sc_z, held, grads, load_sem,
     s_iw, r_iw, s_tw, r_tw, s_iz, r_iz, s_tz, r_tz, s_ix, r_ix, s_ty, r_ty,
     s_bx, r_bx, s_by, r_by, s_bi, r_bi, s_bt, r_bt, s_sn, r_sn, s_sz, r_sz, ready,
 ):
@@ -246,6 +246,8 @@
 
     finish(1, txt_zin, r_bt)
     finish(0, img_zin, r_bi)
+    store = pltpu.make_async_copy(grads, grads_out, load_sem.at[4])
+    store.start()
 
     for copy in pending:
         copy.wait_send()
@@ -257,6 +259,7 @@
     scale = 1.0 / (pairs * pairs)
     result = jnp.sum(sc_near[...], axis=0) * scale
     terms[...] = jnp.where(lane == 1, temp, 1.0) * result
+    store.wait()
 
 
 def write_out(grads, terms, image_grad, text_grad, loss, slope, shift):
@@ -288,7 +291,7 @@
             jax.ShapeDtypeStruct((1, 128), F32),
         ),
         in_specs=[hbm] * 4,
-        out_specs=(vmem, vmem),
+        out_specs=(hbm, vmem),
         scratch_shapes=[
             pltpu.VMEM((2, own, width), F32),
             pltpu.VMEM((2, own, width), F32),
@@ -300,13 +303,14 @@
             pltpu.VMEM((nx * ny * nc, 1, 128), F32),
             pltpu.VMEM((nzh * nzl, 1, 128), F32),
             pltpu.SMEM((2, 1), F32),
-            pltpu.SemaphoreType.DMA((4,)),
+            pltpu.VMEM((2, own, width), F32),
+            pltpu.SemaphoreType.DMA((5,)),
         ] + sems(
             (2,), (2,), (na,), (nn,), (2, nxc), (nw, ny), (2, nxc), (nw, ny), (na,), (nb,), (), ()
         ) + [pltpu.SemaphoreType.REGULAR],
         cost_estimate=pl.CostEstimate(flops=6 * n_pairs * width, bytes_accessed=4 * own * width * 4, transcendentals=2 * n_pairs),
         compiler_params=pltpu.CompilerParams(
-            collective_id=0, has_side_effects=True, vmem_limit_bytes=32 * 1024 * 1024
+            collective_id=0, has_side_effects=True
         ),
     )(images, texts, log_temp, bias)
     one = jax.ShapeDtypeStruct((1, 1), F32)
@@ -316,7 +320,7 @@
         out_shape=(block, block, one, one, one),
         in_specs=[vmem] * 2,
         out_specs=(vmem,) * 5,
-        compiler_params=pltpu.CompilerParams(vmem_limit_bytes=32 * 1024 * 1024),
+        compiler_params=pltpu.CompilerParams(),
     )(grads, terms)
     return image_grad, text_grad, loss[0, 0], slope[0, 0], shift[0, 0]
 

time: 60.8 us -> 60.6 us (level)
  local copies, waits for them, and re-layouts: 1.44 us -> 0 us
  Pallas kernels: 57.1 us -> 58.4 us
    unnamed x4 -> x0, local copies, waits for them, and re-layouts: 1.44 us -> none
    pallas_call x1, Pallas kernels: 0.62 us -> 1.39 us  [on_device(): pl.pallas_call(write_out, out_shape=(block, block, one, one, one), in_spe...]
where the time goes in v7:
time: 60.6 us; the launch traced here: 60.3 us
  Pallas kernels  58.4 us (96%)
  between operations  1.93 us (3%)
    pallas_call x1, Pallas kernels, on_device(): pl.pallas_call(functools.partial(kernel, *factors.values()), out_shape=(j...  57 us
    pallas_call x1, Pallas kernels, on_device(): pl.pallas_call(write_out, out_shape=(block, block, one, one, one), in_spe...  1.39 us

profile of v7, /device:TPU:1, one launch (start us, length us, event | category | flops | bytes accessed | tf_op | source)
XLA Modules:
  0.0 60.3 jit_solution(12135730647558207263)
XLA Ops:
  1.9 57.0 %shard_map.83 = (f32[2,4,1152]{2,1,0:T(4,128)}, f32[1,128]{1,0:T(1,128)}) custom-call(f32[4,1152]{1,0:T(4,128)} %images.1, f32[4,1152]{1,0:T(4,128)} %texts.1, f32[1]{0:T(128)S(6)} %copy.9.log_temp, f32[1]{0:T(128)S(6)} %copy.10.bias), custom_call_target="tpu_custom_call" | custom-call | flops 113246208 | bytes 73728 | tf_op jit(solution)/shard_map/pallas_call | solution.py:287
  58.9 1.4 %shard_map.84 = (f32[4,1152]{1,0:T(4,128)}, f32[4,1152]{1,0:T(4,128)}, f32[1,1]{1,0:T(1,128)}, f32[1,1]{1,0:T(1,128)}, f32[1,1]{1,0:T(1,128)}) custom-call(f32[2,4,1152]{2,1,0:T(4,128)} %get-tuple-element.12.grads, f32[1,128]{1,0:T(1,128)} %get-tuple-element.13.terms), custom_call_target="tpu_custom_call" | custom-call | tf_op jit(solution)/shard_map/pallas_call | solution.py:318
